TPU v7x, 32 devices: a whole 2x2x4 slice. The times are simulated.
32 devices in a mesh: groups: 2 (over y), inst: 4 (over z), tp: 4 (over x, core).
Axes of the slice: x: 2, y: 2, z: 4, core: 2. Of those that a mesh axis runs over, the one named last changes fastest.
Arguments:
- kv_pool: bfloat16 [128, 2, 512, 1024], P(('groups', 'inst'), None, None, 'tp'), parts along dimension 0, may hold values from -16 to 16
- page_table: int32 [64, 8], P(('groups', 'inst')), parts along dimension 0, may hold values from 0 to 15, as said below
- lengths: int32 [64], P(('groups', 'inst')), parts along dimension 0, may hold values from 1 to 4096, as said below
- queries: bfloat16 [64, 2, 8192], P(('groups', 'inst'), None, 'tp'), parts along dimension 0, may hold values from -8 to 8
- new_kv: bfloat16 [64, 2, 2, 1024], P(('groups', 'inst'), None, None, 'tp'), parts along dimension 0, may hold values from -6 to 6
- moves: int32 [8, 2], P('groups'), parts along dimension 0, may hold values from 0 to 31, as said below
Outputs:
- attended: bfloat16 [64, 2, 8192], P(('groups', 'inst'), None, 'tp'), parts along dimension 0
There are 2 independent parts, one for each index of `groups`. A program takes and returns all parts, laid end to end along the dimension named above; each array names one. Nothing has to cross between parts.
Inputs may be any that keep to these rules, and one draw needn't show every extreme that they name: Slot i holds ceil(lengths[i] / 512) cache blocks, listed first in its page table; the blocks of the slots of one instance are distinct; some slot holds exactly 4096 tokens. `page_table`: entries past a slot's block count are valid block numbers of the same pool. The two entries of a move lie on different instances; no slot appears twice in the list; half of the instances hold the cache slots of exactly 2 moves and no hidden slot, the other half exactly 2 hidden slots and no cache slot; no two moves join the same pair of instances.
All inputs are finite; a program needn't handle non-finite values.
Results may differ from a plain program's by a relative error of at most 0.0025.
Values may be sent and summed in bfloat16 or wider, within the bound.
No kernel may reach another device: no remote copies, remote signals or barrier semaphores. Data moves between devices by JAX's collectives and lax.ppermute only.
A program may use at most 64 MiB of HBM per device.

v0:
```python
import functools
import itertools
import math

import jax
import jax.numpy as jnp
from jax import lax
from jax.experimental import pallas as pl
from jax.experimental.pallas import tpu as pltpu
from jax.sharding import PartitionSpec as P

HD = 128
CAP = 2
NEG = -1e30
MAX_HALVES = 6
SMEM = pltpu.SMEM
VMEM = pltpu.VMEM
HBM = pltpu.HBM


class Links:
    def __init__(self, n):
        self.n = n
        half = n // 2
        self.halves = []
        if n % 2 == 0 and math.comb(n, half) <= MAX_HALVES:
            self.halves = list(itertools.combinations(range(n), half))
        self.split = bool(self.halves)
        self.count = half if self.split else n - 1

    def index(self, busy, a, b):
        n = self.n
        if self.split:
            half = n // 2
            rank_a = sum(jnp.where(k < a, busy[k], 0) for k in range(n))
            rank_b = sum(jnp.where(k < b, 1 - busy[k], 0) for k in range(n))
            return lax.rem(rank_a - rank_b + half, half)
        if n & (n - 1) == 0:
            return (a ^ b) - 1
        return lax.rem(a - b + n, n) - 1

    def branch(self, busy):
        mask = sum(busy[k] << k for k in range(self.n))
        return sum(
            jnp.where(mask == sum(1 << i for i in half), k, 0) for k, half in enumerate(self.halves)
        )

    def forward(self, which, j):
        n = self.n
        if self.split:
            busy = self.halves[which]
            spare = [i for i in range(n) if i not in busy]
            return [(s, busy[(k + j) % len(busy)]) for k, s in enumerate(spare)]
        if n & (n - 1) == 0:
            return [(i, i ^ (j + 1)) for i in range(n)]
        return [(i, (i + j + 1) % n) for i in range(n)]

    def backward(self, which, j):
        return [(b, a) for a, b in self.forward(which, j)]

    def both(self, pairs):
        return sorted(set(pairs) | {(b, a) for a, b in pairs}) if self.split else pairs


def find_moves(links, moves, rows_inst, me, hidden=None, rank=None, slot=None):
    n = links.n
    count = links.count
    for j in range(count + 1):
        if hidden is not None:
            hidden[j] = -1
        if rank is not None:
            rank[j] = CAP
    if slot is not None:
        for c in range(CAP + 1):
            slot[c] = -1
    total = moves.shape[1]
    busy = None
    if links.split:
        froms = [moves[0, m] // rows_inst for m in range(total)]
        busy = [
            functools.reduce(jnp.bitwise_or, [(f == k).astype(jnp.int32) for f in froms]) for k in range(n)
        ]

    def step(m, seen):
        cache_slot = moves[0, m]
        hidden_slot = moves[1, m]
        from_inst = cache_slot // rows_inst
        to_inst = hidden_slot // rows_inst
        index = links.index(busy, from_inst, to_inst)
        if hidden is not None:
            hidden[jnp.where(to_inst == me, index, count)] = lax.rem(hidden_slot, rows_inst)
        mine = from_inst == me
        if rank is not None:
            rank[jnp.where(mine, index, count)] = seen
        if slot is not None:
            slot[jnp.where(mine, seen, CAP)] = lax.rem(cache_slot, rows_inst)
        return jnp.where(mine, seen + 1, seen)

    if links.split:
        seen = jnp.int32(0)
        for m in range(total):
            seen = step(m, seen)
    else:
        lax.fori_loop(0, total, step, jnp.int32(0))
    return busy


def pack_kernel(links, moves_hbm, q_hbm, kv_hbm, *refs):
    outs = refs[: links.count]
    branch, hidden, moves, q, kv, sems = refs[links.count :]
    copies = [
        pltpu.make_async_copy(moves_hbm, moves, sems.at[0]),
        pltpu.make_async_copy(q_hbm, q, sems.at[1]),
        pltpu.make_async_copy(kv_hbm, kv, sems.at[2]),
    ]
    for c in copies:
        c.start()
    rows_inst, heads, _ = q.shape
    me = lax.axis_index("inst")
    copies[0].wait()
    busy = find_moves(links, moves, rows_inst, me, hidden=hidden)
    branch[0] = links.branch(busy) if links.split else 0
    copies[1].wait()
    copies[2].wait()
    for j, out in enumerate(outs):
        row = jnp.maximum(hidden[j], 0)
        out[0:heads, :] = q[row]
        out[heads:, :] = kv[row]


def set_row(at, rows, fresh, qbd, fk, fv, groups):
    heads, hd = rows.shape
    per = heads // groups
    zero = jnp.zeros((per, hd), jnp.bfloat16)
    for g in range(groups):
        for k in range(groups):
            qbd[at, g * per : (g + 1) * per, k * hd : (k + 1) * hd] = (
                rows[g * per : (g + 1) * per] if k == g else zero
            )
    if fk is None:
        return
    fresh = fresh.astype(jnp.float32)
    token = lax.broadcasted_iota(jnp.int32, (16, hd), 0)
    for plane, ref in enumerate((fk, fv)):
        for g in range(groups):
            block = jnp.zeros((16, hd), jnp.float32)
            for u in range(fresh.shape[0] // (2 * groups)):
                line = (u * groups + g) * 2 + plane
                block = jnp.where(token == u, fresh[line : line + 1], block)
            ref[at, 0:16, g * hd : (g + 1) * hd] = block.astype(jnp.bfloat16)


def attend_list(rows, chunk, steps, lists, count, buf, qbd, fk, fv, scores, new, part_max, top, part_sum, acc):
    page, owner, limit = lists
    _, heads, columns = qbd.shape
    hd = acc.shape[2]
    groups = columns // hd
    per = heads // groups
    block = buf.shape[2]
    factor = math.log2(math.e) / math.sqrt(hd)
    loops = lax.div(count + (chunk - 1), jnp.int32(chunk))
    keys_of = (((1,), (1,)), ((), ()))
    values_of = (((1,), (0,)), ((), ()))
    lane = lax.broadcasted_iota(jnp.int32, (heads, block), 1)
    token = lax.broadcasted_iota(jnp.int32, (heads, hd), 1)
    seen = token <= lax.broadcasted_iota(jnp.int32, (heads, hd), 0) % steps

    def diagonal(o):
        return jnp.concatenate(
            [o[g * per : (g + 1) * per, g * hd : (g + 1) * hd] for g in range(groups)], axis=0
        )

    def first(k):
        r = owner[k]
        s = lax.dot_general(qbd[r], buf[page[k], 0], keys_of, preferred_element_type=jnp.float32)
        s = jnp.where(lane < limit[k], s, NEG)
        scores[k] = s
        m = s[:, 0:hd]
        for c in range(1, block // hd):
            m = jnp.maximum(m, s[:, c * hd : (c + 1) * hd])
        part_max[r] = jnp.maximum(part_max[r], m)

    def second(k):
        r = owner[k]
        m = top[r]
        pieces = []
        total = jnp.zeros((heads, hd), jnp.float32)
        for c in range(block // hd):
            e = jnp.exp2((scores[k, :, c * hd : (c + 1) * hd] - m) * factor)
            total = total + e
            pieces.append(e.astype(jnp.bfloat16))
        o = lax.dot_general(
            jnp.concatenate(pieces, axis=1), buf[page[k], 1], values_of, preferred_element_type=jnp.float32
        )
        part_sum[r] = part_sum[r] + total
        acc[r] = acc[r] + diagonal(o)

    def others(do):
        def step(i, carry):
            for j in range(chunk):
                do(i * chunk + j)
            return carry

        lax.fori_loop(1, loops, step, 0)

    for r in range(rows):
        s = lax.dot_general(qbd[r], fk[r], keys_of, preferred_element_type=jnp.float32)
        s = jnp.where(seen, s, NEG)
        new[r] = s
        part_max[r] = s
    part_max[rows] = jnp.zeros((heads, hd), jnp.float32)
    for j in range(chunk):
        first(j)
    others(first)

    top[rows] = jnp.zeros((heads, hd), jnp.float32)
    part_sum[rows] = jnp.zeros((heads, hd), jnp.float32)
    acc[rows] = jnp.zeros((heads, hd), jnp.float32)
    for r in range(rows):
        m = jnp.broadcast_to(jnp.max(part_max[r], axis=1, keepdims=True), (heads, hd))
        top[r] = m
        e = jnp.exp2((new[r] - m) * factor)
        part_sum[r] = e
        acc[r] = diagonal(
            lax.dot_general(e.astype(jnp.bfloat16), fv[r], values_of, preferred_element_type=jnp.float32)
        )
    for j in range(chunk):
        second(j)
    others(second)
    for r in range(rows):
        acc[r] = acc[r] / jnp.sum(part_sum[r], axis=1, keepdims=True)


def list_kernel(links, chunk, far_chunk, fetches, moves_hbm, page_hbm, length_hbm, q_hbm, kv_hbm, pool, *refs):
    (
        buf, qbd, fk, fv, hidden, rank, slot,
        page, owner, limit, counts, far_page, far_owner, far_limit,
        moves, page_table, lengths, q, kv, small_sems, sems,
    ) = refs
    rows_inst, heads, hd = q.shape
    slots, _, block, columns = pool.shape
    groups = columns // hd
    me = lax.axis_index("inst")

    small = [
        pltpu.make_async_copy(src, dst, small_sems.at[i])
        for i, (src, dst) in enumerate(
            [(moves_hbm, moves), (page_hbm, page_table), (length_hbm, lengths), (q_hbm, q), (kv_hbm, kv)]
        )
    ]
    for c in small:
        c.start()

    part = slots // fetches

    def fetch(k, plane):
        at = pl.ds(k * part, part)
        return pltpu.make_async_copy(pool.at[at, plane], buf.at[at, plane], sems.at[k, plane])

    for plane in range(2):
        for k in range(fetches):
            fetch(k, plane).start()

    fk[...] = jnp.zeros(fk.shape, fk.dtype)
    fv[...] = jnp.zeros(fv.shape, fv.dtype)
    for c in small:
        c.wait()
    find_moves(links, moves, rows_inst, me, hidden=hidden, rank=rank, slot=slot)

    def row(r, counts):
        near, far = counts
        length = lengths[r]
        which = jnp.int32(CAP)
        for c in range(CAP):
            which = jnp.where(slot[c] == r, c, which)
        moved = which < CAP

        def one(b, counts):
            near, far = counts
            number = page_table[r, b]
            left = length - b * block
            at = jnp.where(moved, slots + far_chunk, near)
            page[at] = number
            owner[at] = r
            limit[at] = left
            at = jnp.where(moved, far, slots + far_chunk)
            far_page[at] = number
            far_owner[at] = which
            far_limit[at] = left
            return jnp.where(moved, near, near + 1), jnp.where(moved, far + 1, far)

        return lax.fori_loop(0, lax.div(length + (block - 1), jnp.int32(block)), one, (near, far))

    near, far = lax.fori_loop(0, rows_inst, row, (jnp.int32(0), jnp.int32(0)))
    counts[0] = near
    counts[1] = far
    for j in range(chunk):
        page[near + j] = 0
        owner[near + j] = rows_inst
        limit[near + j] = 0
    for j in range(far_chunk):
        far_page[far + j] = 0
        far_owner[far + j] = CAP
        far_limit[far + j] = 0

    for r in range(rows_inst):
        set_row(r, q[r], kv[r], qbd, fk, fv, groups)
    set_row(rows_inst, q[0], None, qbd, None, None, groups)

    for plane in range(2):
        for k in range(fetches):
            fetch(k, plane).wait()


def stay_kernel(chunk, steps, slot, page, owner, limit, counts, buf, qbd, fk, fv, order, local, *work):
    rows_inst = local.shape[0]
    attend_list(rows_inst, chunk, steps, (page, owner, limit), counts[0], buf, qbd, fk, fv, *work)
    acc = work[-1]
    for r in range(rows_inst):
        vacant = functools.reduce(jnp.logical_or, [slot[c] == r for c in range(CAP)])
        local[r] = jnp.where(vacant, 0.0, acc[r]).astype(jnp.bfloat16)


def moved_kernel(links, chunk, steps, rank, far_page, far_owner, far_limit, counts, buf, *refs):
    recv, back = refs[: links.count], refs[links.count : 2 * links.count]
    qbd, fk, fv, *work = refs[2 * links.count :]
    acc = work[-1]
    heads = qbd.shape[1]
    groups = qbd.shape[2] // acc.shape[2]
    count = counts[1]

    @pl.when(count > 0)
    def _():
        fk[:, 16:, :] = jnp.zeros((CAP, fk.shape[1] - 16, fk.shape[2]), fk.dtype)
        fv[:, 16:, :] = jnp.zeros((CAP, fv.shape[1] - 16, fv.shape[2]), fv.dtype)
        for j in range(links.count):

            def put(j=j):
                set_row(rank[j], recv[j][0:heads, :], recv[j][heads:, :], qbd, fk, fv, groups)

            if links.count == CAP:
                put()
            else:
                pl.when(rank[j] < CAP)(put)
        attend_list(
            CAP, chunk, steps, (far_page, far_owner, far_limit), count,
            buf, qbd, fk, fv, *work,
        )
        for j in range(links.count):
            back[j][...] = acc[rank[j]].astype(jnp.bfloat16)


def place_kernel(links, hidden, local, *refs):
    back, (out, staged, sem) = refs[: links.count], refs[links.count :]
    staged[...] = local[...]
    for j in range(links.count):

        @pl.when(hidden[j] >= 0)
        def _():
            staged[hidden[j]] = back[j][...]

    write = pltpu.make_async_copy(staged, out, sem)
    write.start()
    write.wait()


def body(kv_pool, page_table, lengths, queries, new_kv, moves):
    links = Links(lax.axis_size("inst"))
    rows_inst, steps, width = queries.shape
    slots, _, block, columns = kv_pool.shape
    groups = columns // HD
    heads_all = width // HD
    heads = steps * heads_all
    fresh_rows = steps * groups * 2
    bf16 = jnp.bfloat16
    f32 = jnp.float32
    i32 = jnp.int32
    q = queries.reshape(rows_inst, steps, heads_all, HD).transpose(0, 2, 1, 3).reshape(rows_inst, heads, HD)
    kv = (
        new_kv.reshape(rows_inst, steps, 2, groups, HD)
        .transpose(0, 1, 3, 2, 4)
        .reshape(rows_inst, fresh_rows, HD)
    )
    smem = pl.BlockSpec(memory_space=SMEM)
    vmem = pl.BlockSpec(memory_space=VMEM)
    hbm = pl.BlockSpec(memory_space=HBM)
    in_hbm = lambda x: pltpu.with_memory_space_constraint(x, HBM)
    move_cols = moves.T
    count = links.count
    chunk = 4
    far_chunk = 5
    fetches = math.gcd(slots, 4)
    mib = 1024 * 1024

    *packed, branch = pl.pallas_call(
        functools.partial(pack_kernel, links),
        out_shape=[jax.ShapeDtypeStruct((heads + fresh_rows, HD), bf16)] * count
        + [SMEM((1,), i32)],
        in_specs=[hbm, hbm, hbm],
        out_specs=[vmem] * count + [smem],
        scratch_shapes=[
            SMEM((count + 1,), i32),
            SMEM(move_cols.shape, i32),
            VMEM(q.shape, bf16),
            VMEM(kv.shape, bf16),
            pltpu.SemaphoreType.DMA((3,)),
        ],
        compiler_params=pltpu.CompilerParams(vmem_limit_bytes=4 * mib),
        name="pack",
    )(in_hbm(move_cols), in_hbm(q), in_hbm(kv))

    def rows_state(rows):
        return [
            VMEM((rows + 1, heads, columns), bf16),
            VMEM((rows, HD, columns), bf16),
            VMEM((rows, HD, columns), bf16),
        ]

    def work_state(rows):
        return [
            VMEM((slots + far_chunk, heads, block), f32),
            VMEM((rows, heads, HD), f32),
        ] + [VMEM((rows + 1, heads, HD), f32)] * 4

    anyspace = pl.BlockSpec(memory_space=pl.ANY)
    blocks = SMEM((slots + far_chunk + 1,), i32)
    staged = VMEM((rows_inst, heads, HD), bf16)

    def exchange(arrays, ways):
        done = {j: lax.ppermute(arrays[j], "inst", ways[j]) for j in reversed(range(count))}
        return [done[j] for j in range(count)]

    def rest(which, kv_pool, page_table, lengths, q, kv, move_cols, *packed):
        ways = [links.forward(which, j) for j in range(count)]
        received = exchange(packed, [links.both(way) for way in ways])
        (
            buf, qbd, fk, fv, hidden, rank, slot,
            page, owner, limit, counts, far_page, far_owner, far_limit,
        ) = pl.pallas_call(
            functools.partial(list_kernel, links, chunk, far_chunk, fetches),
            out_shape=[VMEM(kv_pool.shape, bf16)]
            + rows_state(rows_inst)
            + [SMEM((count + 1,), i32), SMEM((count + 1,), i32), SMEM((CAP + 1,), i32)]
            + [blocks, blocks, blocks, SMEM((2,), i32), blocks, blocks, blocks],
            in_specs=[hbm] * 6,
            out_specs=[vmem] * 4 + [smem] * 10,
            scratch_shapes=[
                SMEM(move_cols.shape, i32),
                SMEM(page_table.shape, i32),
                SMEM(lengths.shape, i32),
                VMEM(q.shape, bf16),
                VMEM(kv.shape, bf16),
                pltpu.SemaphoreType.DMA((5,)),
                pltpu.SemaphoreType.DMA((fetches, 2)),
            ],
            compiler_params=pltpu.CompilerParams(vmem_limit_bytes=16 * mib),
            cost_estimate=pl.CostEstimate(flops=2**27, bytes_accessed=2**23, transcendentals=2**18),
            name="list",
        )(*map(in_hbm, (move_cols, page_table, lengths, q, kv, kv_pool)))
        back = pl.pallas_call(
            functools.partial(moved_kernel, links, far_chunk, steps),
            out_shape=[jax.ShapeDtypeStruct((heads, HD), bf16)] * count,
            in_specs=[smem] * 5 + [vmem] + [vmem] * count,
            out_specs=[vmem] * count,
            scratch_shapes=rows_state(CAP) + work_state(CAP),
            compiler_params=pltpu.CompilerParams(vmem_limit_bytes=16 * mib),
            name="moved",
        )(rank, far_page, far_owner, far_limit, counts, buf, *received)
        returned = exchange(back, [links.backward(which, j) for j in range(count)])
        local = pl.pallas_call(
            functools.partial(stay_kernel, chunk, steps),
            out_shape=staged,
            in_specs=[smem] * 5 + [vmem] * 4 + [anyspace],
            out_specs=vmem,
            scratch_shapes=work_state(rows_inst),
            compiler_params=pltpu.CompilerParams(vmem_limit_bytes=16 * mib),
            cost_estimate=pl.CostEstimate(flops=2**27, bytes_accessed=2**23, transcendentals=2**18),
            name="stay",
        )(slot, page, owner, limit, counts, buf, qbd, fk, fv, back[0])
        out = pl.pallas_call(
            functools.partial(place_kernel, links),
            out_shape=HBM((rows_inst, heads, HD), bf16),
            in_specs=[smem, vmem] + [vmem] * count,
            out_specs=hbm,
            scratch_shapes=[staged, pltpu.SemaphoreType.DMA],
            compiler_params=pltpu.CompilerParams(vmem_limit_bytes=4 * mib),
            name="place",
        )(hidden, local, *returned)
        out = out.reshape(rows_inst, heads_all, steps, HD).transpose(0, 2, 1, 3)
        return out.reshape(rows_inst, steps, width)

    operands = (kv_pool, page_table, lengths, q, kv, move_cols, *packed)
    if links.split:
        return lax.switch(
            branch[0], [functools.partial(rest, k) for k in range(len(links.halves))], *operands
        )
    return rest(0, *operands)


def solution(mesh):
    placed = (
        P(("groups", "inst"), None, None, "tp"),
        P(("groups", "inst"), None),
        P(("groups", "inst")),
        P(("groups", "inst"), None, "tp"),
        P(("groups", "inst"), None, None, "tp"),
        P("groups", None),
    )
    return jax.shard_map(
        body,
        mesh=mesh,
        in_specs=placed,
        out_specs=P(("groups", "inst"), None, "tp"),
        check_vma=False,
    )
```

profile of v0, /device:TPU:0, one launch (start us, length us, event | category | flops | bytes accessed | tf_op | source)
XLA Modules:
  0.0 20.4 jit_solution(9567736614243567201)
XLA Ops:
  0.0 0.9 %pack.1 = (bf16[40,128]{1,0:T(8,128)(2,1)S(1)}, bf16[40,128]{1,0:T(8,128)(2,1)S(1)}, s32[1]{0:T(128)S(4)}) custom-call(s32[2,4]{1,0:T(2,128)} %bitcast.62, bf16[8,32,128]{2,1,0:T(8,128)(2,1)} %bitcast.42, bf16[8,8,128]{2,1,0:T(8,128)(2,1)} %bitcast.49), custom_call_target="tpu_custom_call" | custom-call | tf_op jit(solution)/shard_map/pack/pallas_call | solution.py:395
  0.9 19.3 %conditional.1 = (bf16[8,2,2048]{2,1,0:T(2,128)(2,1)}) conditional(s32[]{:T(128)} %bitcast.37, (s32[2,4]{1,0:T(2,128)}, s32[8,8]{1,0:T(8,128)}, s32[8]{0:T(128)}, bf16[8,32,128]{2,1,0:T(8,128)(2,1)}, bf16[8,8,128]{2,1,0:T(8,128)(2,1)}, /*index=5*/bf16[16,2,512,256]{3,2,1,0:T(8,128)(2,1)}, ...), branch_computations={%region_0.0_spmd, %region_1.0_spmd, %region_2.0_spmd, %region_3.0_... | conditional | flops 268435456 | bytes 16924840 | solution.py:494
  1.1 4.1 %collective-permute-start.20 = (bf16[40,128]{1,0:T(8,128)(2,1)S(1)}, bf16[40,128]{1,0:T(8,128)(2,1)S(1)}, u32[]{:S(2)}, u32[]{:S(2)}) collective-permute-start(bf16[40,128]{1,0:T(8,128)(2,1)S(1)} %get-tuple-element.248), channel_id=1, source_target_pairs={{0,8},{4,12},{8,0},{12,4},{1,9},{5,13},{9,1},{13,5},{2,10},{6,14},... | collective-permute-start | bytes 30728 | tf_op jit(solution)/shard_map/cond/branch_5_fun/ppermute | solution.py:430
  5.2 1.3 %collective-permute-start.21 = (bf16[40,128]{1,0:T(8,128)(2,1)S(1)}, bf16[40,128]{1,0:T(8,128)(2,1)S(1)}, u32[]{:S(2)}, u32[]{:S(2)}) collective-permute-start(bf16[40,128]{1,0:T(8,128)(2,1)S(1)} %get-tuple-element.249), channel_id=1, source_target_pairs={{0,12},{4,8},{8,4},{12,0},{1,13},{5,9},{9,5},{13,1},{2,14},{6,10},... | collective-permute-start | bytes 30728 | tf_op jit(solution)/shard_map/cond/branch_5_fun/ppermute | solution.py:430
  6.6 3.6 %list.11 = (bf16[16,2,512,256]{3,2,1,0:T(8,128)(2,1)S(1)}, bf16[9,32,256]{2,1,0:T(8,128)(2,1)S(1)}, bf16[8,128,256]{2,1,0:T(8,128)(2,1)S(1)}, bf16[8,128,256]{2,...) custom-call(s32[2,4]{1,0:T(2,128)} %get-tuple-element.228.moves_hbm,, ...), custom_call_target="tpu_custom_call" | custom-call | flops 134217728 | bytes 8388608 | tf_op jit(solution)/shard_map/cond/branch_5_fun/list/pallas_call | solution.py:439
  10.2 0.0 collective-permute-done.20.refs_0_
  10.2 0.5 %collective-permute-done.21.refs_1_ = bf16[40,128]{1,0:T(8,128)(2,1)S(1)} collective-permute-done((bf16[40,128]{1,0:T(8,128)(2,1)S(1)}, bf16[40,128]{1,0:T(8,128)(2,1)S(1)}, u32[]{:S(2)}, u32[]{:S(2)}) %collective-permute-start.21) | collective-permute-done | bytes 10272 | tf_op jit(solution)/shard_map/cond/branch_5_fun/ppermute | solution.py:430
  10.7 1.3 %collective-permute-start.22 = (bf16[32,128]{1,0:T(8,128)(2,1)S(1)}, bf16[32,128]{1,0:T(8,128)(2,1)S(1)}, u32[]{:S(2)}, u32[]{:S(2)}) collective-permute-start(bf16[32,128]{1,0:T(8,128)(2,1)S(1)} %get-tuple-element.250.order), channel_id=1, source_target_pairs={{8,0},{12,4},{9,1},{13,5},{10,2},{14,6},{11,3},{15,7},{24,16},{28,... | collective-permute-start | bytes 24584 | tf_op jit(solution)/shard_map/cond/branch_5_fun/ppermute | solution.py:430
  12.0 1.3 %collective-permute-start.23 = (bf16[32,128]{1,0:T(8,128)(2,1)S(1)}, bf16[32,128]{1,0:T(8,128)(2,1)S(1)}, u32[]{:S(2)}, u32[]{:S(2)}) collective-permute-start(bf16[32,128]{1,0:T(8,128)(2,1)S(1)} %get-tuple-element.251), channel_id=1, source_target_pairs={{12,0},{8,4},{13,1},{9,5},{14,2},{10,6},{15,3},{11,7},{28,16},{24,... | collective-permute-start | bytes 24584 | tf_op jit(solution)/shard_map/cond/branch_5_fun/ppermute | solution.py:430
  13.3 1.9 %stay.11.local = bf16[8,32,128]{2,1,0:T(8,128)(2,1)S(1)} custom-call(s32[3]{0:T(128)S(4)} %get-tuple-element.235.slot, s32[22]{0:T(128)S(4)} %get-tuple-element.236.page, s32[22]{0:T(128)S(4)} %get-tuple-element.237.owner, s32[22]{0:T(128)S(4)} %get-tuple-element.238.limit, s32[2]{0:T(128)S(4)} %get-tuple-element.239.counts, ...), custom_call_target="tpu_custom_call" | custom-call | flops 134217728 | bytes 8388608 | tf_op jit(solution)/shard_map/cond/branch_5_fun/stay/pallas_call | solution.py:470
  15.2 1.9 %collective-permute-done.22.refs_0_ = bf16[32,128]{1,0:T(8,128)(2,1)S(1)} collective-permute-done((bf16[32,128]{1,0:T(8,128)(2,1)S(1)}, bf16[32,128]{1,0:T(8,128)(2,1)S(1)}, u32[]{:S(2)}, u32[]{:S(2)}) %collective-permute-start.22) | collective-permute-done | bytes 8224 | tf_op jit(solution)/shard_map/cond/branch_5_fun/ppermute | solution.py:430
  17.1 2.2 %collective-permute-done.23.refs_1_ = bf16[32,128]{1,0:T(8,128)(2,1)S(1)} collective-permute-done((bf16[32,128]{1,0:T(8,128)(2,1)S(1)}, bf16[32,128]{1,0:T(8,128)(2,1)S(1)}, u32[]{:S(2)}, u32[]{:S(2)}) %collective-permute-start.23) | collective-permute-done | bytes 8224 | tf_op jit(solution)/shard_map/cond/branch_5_fun/ppermute | solution.py:430
  19.3 0.6 %place.11 = bf16[8,32,128]{2,1,0:T(8,128)(2,1)} custom-call(s32[3]{0:T(128)S(4)} %get-tuple-element.234.hidden, bf16[8,32,128]{2,1,0:T(8,128)(2,1)S(1)} %stay.11.local, bf16[32,128]{1,0:T(8,128)(2,1)S(1)} %collective-permute-done.22.refs_0_, bf16[32,128]{1,0:T(8,128)(2,1)S(1)} %collective-permute-done.23.refs_1_), custom_call_target="tpu_custom_call" | custom-call | tf_op jit(solution)/shard_map/cond/branch_5_fun/place/pallas_call | solution.py:480
  (1 shorter events, 0.0 us)
Async XLA Ops:
  1.1 9.1 %collective-permute-start.20 = (bf16[40,128]{1,0:T(8,128)(2,1)S(1)}, bf16[40,128]{1,0:T(8,128)(2,1)S(1)}, u32[]{:S(2)}, u32[]{:S(2)}) collective-permute-start(bf16[40,128]{1,0:T(8,128)(2,1)S(1)} %get-tuple-element.248), channel_id=1, source_target_pairs={{0,8},{4,12},{8,0},{12,4},{1,9},{5,13},{9,1},{13,5},{2,10},{6,14},... | collective-permute-start | bytes 30728 | tf_op jit(solution)/shard_map/cond/branch_5_fun/ppermute | solution.py:430
  5.2 5.5 %collective-permute-start.21 = (bf16[40,128]{1,0:T(8,128)(2,1)S(1)}, bf16[40,128]{1,0:T(8,128)(2,1)S(1)}, u32[]{:S(2)}, u32[]{:S(2)}) collective-permute-start(bf16[40,128]{1,0:T(8,128)(2,1)S(1)} %get-tuple-element.249), channel_id=1, source_target_pairs={{0,12},{4,8},{8,4},{12,0},{1,13},{5,9},{9,5},{13,1},{2,14},{6,10},... | collective-permute-start | bytes 30728 | tf_op jit(solution)/shard_map/cond/branch_5_fun/ppermute | solution.py:430
  10.7 6.4 %collective-permute-start.22 = (bf16[32,128]{1,0:T(8,128)(2,1)S(1)}, bf16[32,128]{1,0:T(8,128)(2,1)S(1)}, u32[]{:S(2)}, u32[]{:S(2)}) collective-permute-start(bf16[32,128]{1,0:T(8,128)(2,1)S(1)} %get-tuple-element.250.order), channel_id=1, source_target_pairs={{8,0},{12,4},{9,1},{13,5},{10,2},{14,6},{11,3},{15,7},{24,16},{28,... | collective-permute-start | bytes 24584 | tf_op jit(solution)/shard_map/cond/branch_5_fun/ppermute | solution.py:430
  12.0 7.3 %collective-permute-start.23 = (bf16[32,128]{1,0:T(8,128)(2,1)S(1)}, bf16[32,128]{1,0:T(8,128)(2,1)S(1)}, u32[]{:S(2)}, u32[]{:S(2)}) collective-permute-start(bf16[32,128]{1,0:T(8,128)(2,1)S(1)} %get-tuple-element.251), channel_id=1, source_target_pairs={{12,0},{8,4},{13,1},{9,5},{14,2},{10,6},{15,3},{11,7},{28,16},{24,... | collective-permute-start | bytes 24584 | tf_op jit(solution)/shard_map/cond/branch_5_fun/ppermute | solution.py:430
where the time goes:
time: 20.2 us; the launch traced here: 20.4 us
  starting transfers between devices  8.02 us (40%)
  Pallas kernels  7.03 us (35%)
  waiting for transfers between devices  4.63 us (23%)
  loops' own time  0.49 us (2%)
    ppermute x4, starting transfers between devices, exchange(): lax.ppermute(arrays[j], 'inst', ways[j])  8.02 us
    ppermute x4, waiting for transfers between devices, exchange(): lax.ppermute(arrays[j], 'inst', ways[j])  4.63 us
    pallas_call x1, Pallas kernels, rest(): pl.pallas_call(functools.partial(list_kernel, links, chunk, far_chunk, fe...  3.61 us
    pallas_call x1, Pallas kernels, rest(): pl.pallas_call(functools.partial(stay_kernel, chunk, steps), out_shape=st...  1.91 us
    pallas_call x1, Pallas kernels, body(): pl.pallas_call(functools.partial(pack_kernel, links), out_shape=[jax.Shap...  0.87 us
    pallas_call x1, Pallas kernels, rest(): pl.pallas_call(functools.partial(place_kernel, links), out_shape=HBM((row...  0.64 us
    another operation x1, loops' own time, body(): lax.switch(branch[0], [functools.partial(rest, k) for k in range(len(link...  0.49 us
  transfers between devices with their start and end apart: 4, of which 3 were waited for; matrix products, arithmetic and copies ran while one was open for 0% of the time, Pallas kernels for 27%

commit v1 on v0

--- a/solution.py
+++ b/solution.py
@@ -34,7 +34,7 @@
             half = n // 2
             rank_a = sum(jnp.where(k < a, busy[k], 0) for k in range(n))
             rank_b = sum(jnp.where(k < b, 1 - busy[k], 0) for k in range(n))
-            return lax.rem(rank_a - rank_b + half, half)
+            return half - 1 - lax.rem(rank_a - rank_b + half, half)
         if n & (n - 1) == 0:
             return (a ^ b) - 1
         return lax.rem(a - b + n, n) - 1
@@ -50,7 +50,8 @@
         if self.split:
             busy = self.halves[which]
             spare = [i for i in range(n) if i not in busy]
-            return [(s, busy[(k + j) % len(busy)]) for k, s in enumerate(spare)]
+            shift = self.count - 1 - j
+            return [(s, busy[(k + shift) % len(busy)]) for k, s in enumerate(spare)]
         if n & (n - 1) == 0:
             return [(i, i ^ (j + 1)) for i in range(n)]
         return [(i, (i + j + 1) % n) for i in range(n)]
@@ -105,9 +106,14 @@
     return busy
 
 
-def pack_kernel(links, moves_hbm, q_hbm, kv_hbm, *refs):
+def fetch(pool, buf, sems, part, k, plane):
+    at = pl.ds(k * part, part)
+    return pltpu.make_async_copy(pool.at[at, plane], buf.at[at, plane], sems.at[k, plane])
+
+
+def pack_kernel(links, part, moves_hbm, q_hbm, kv_hbm, pool, *refs):
     outs = refs[: links.count]
-    branch, hidden, moves, q, kv, sems = refs[links.count :]
+    branch, buf, hidden, moves, q, kv, sems, pool_sems = refs[links.count :]
     copies = [
         pltpu.make_async_copy(moves_hbm, moves, sems.at[0]),
         pltpu.make_async_copy(q_hbm, q, sems.at[1]),
@@ -115,6 +121,8 @@
     ]
     for c in copies:
         c.start()
+    for plane in range(2):
+        fetch(pool, buf, pool_sems, part, 0, plane).start()
     rows_inst, heads, _ = q.shape
     me = lax.axis_index("inst")
     copies[0].wait()
@@ -126,6 +134,8 @@
         row = jnp.maximum(hidden[j], 0)
         out[0:heads, :] = q[row]
         out[heads:, :] = kv[row]
+    for plane in range(2):
+        fetch(pool, buf, pool_sems, part, 0, plane).wait()
 
 
 def set_row(at, rows, fresh, qbd, fk, fv, groups):
@@ -150,7 +160,7 @@
             ref[at, 0:16, g * hd : (g + 1) * hd] = block.astype(jnp.bfloat16)
 
 
-def attend_list(rows, chunk, steps, lists, count, buf, qbd, fk, fv, scores, new, part_max, top, part_sum, acc):
+def attend_list(rows, ahead, chunk, steps, lists, count, buf, qbd, fk, fv, scores, new, part_max, top, part_sum, acc):
     page, owner, limit = lists
     _, heads, columns = qbd.shape
     hd = acc.shape[2]
@@ -158,7 +168,7 @@
     per = heads // groups
     block = buf.shape[2]
     factor = math.log2(math.e) / math.sqrt(hd)
-    loops = lax.div(count + (chunk - 1), jnp.int32(chunk))
+    loops = lax.div(count - ahead + (chunk - 1), jnp.int32(chunk))
     keys_of = (((1,), (1,)), ((), ()))
     values_of = (((1,), (0,)), ((), ()))
     lane = lax.broadcasted_iota(jnp.int32, (heads, block), 1)
@@ -198,10 +208,10 @@
     def others(do):
         def step(i, carry):
             for j in range(chunk):
-                do(i * chunk + j)
+                do(ahead + i * chunk + j)
             return carry
 
-        lax.fori_loop(1, loops, step, 0)
+        lax.fori_loop(0, loops, step, 0)
 
     for r in range(rows):
         s = lax.dot_general(qbd[r], fk[r], keys_of, preferred_element_type=jnp.float32)
@@ -209,7 +219,7 @@
         new[r] = s
         part_max[r] = s
     part_max[rows] = jnp.zeros((heads, hd), jnp.float32)
-    for j in range(chunk):
+    for j in range(ahead):
         first(j)
     others(first)
 
@@ -224,14 +234,14 @@
         acc[r] = diagonal(
             lax.dot_general(e.astype(jnp.bfloat16), fv[r], values_of, preferred_element_type=jnp.float32)
         )
-    for j in range(chunk):
+    for j in range(ahead):
         second(j)
     others(second)
     for r in range(rows):
         acc[r] = acc[r] / jnp.sum(part_sum[r], axis=1, keepdims=True)
 
 
-def list_kernel(links, chunk, far_chunk, fetches, moves_hbm, page_hbm, length_hbm, q_hbm, kv_hbm, pool, *refs):
+def list_kernel(links, chunk, far_chunk, part, moves_hbm, page_hbm, length_hbm, q_hbm, kv_hbm, pool, begun, *refs):
     (
         buf, qbd, fk, fv, hidden, rank, slot,
         page, owner, limit, counts, far_page, far_owner, far_limit,
@@ -251,15 +261,9 @@
     for c in small:
         c.start()
 
-    part = slots // fetches
-
-    def fetch(k, plane):
-        at = pl.ds(k * part, part)
-        return pltpu.make_async_copy(pool.at[at, plane], buf.at[at, plane], sems.at[k, plane])
-
-    for plane in range(2):
-        for k in range(fetches):
-            fetch(k, plane).start()
+    rest = [(k, plane) for plane in range(2) for k in range(1, slots // part)]
+    for k, plane in rest:
+        fetch(pool, buf, sems, part, k, plane).start()
 
     fk[...] = jnp.zeros(fk.shape, fk.dtype)
     fv[...] = jnp.zeros(fv.shape, fv.dtype)
@@ -307,21 +311,20 @@
         set_row(r, q[r], kv[r], qbd, fk, fv, groups)
     set_row(rows_inst, q[0], None, qbd, None, None, groups)
 
-    for plane in range(2):
-        for k in range(fetches):
-            fetch(k, plane).wait()
+    for k, plane in rest:
+        fetch(pool, buf, sems, part, k, plane).wait()
 
 
 def stay_kernel(chunk, steps, slot, page, owner, limit, counts, buf, qbd, fk, fv, order, local, *work):
     rows_inst = local.shape[0]
-    attend_list(rows_inst, chunk, steps, (page, owner, limit), counts[0], buf, qbd, fk, fv, *work)
+    attend_list(rows_inst, chunk, chunk, steps, (page, owner, limit), counts[0], buf, qbd, fk, fv, *work)
     acc = work[-1]
     for r in range(rows_inst):
         vacant = functools.reduce(jnp.logical_or, [slot[c] == r for c in range(CAP)])
         local[r] = jnp.where(vacant, 0.0, acc[r]).astype(jnp.bfloat16)
 
 
-def moved_kernel(links, chunk, steps, rank, far_page, far_owner, far_limit, counts, buf, *refs):
+def moved_kernel(links, ahead, chunk, steps, rank, far_page, far_owner, far_limit, counts, buf, *refs):
     recv, back = refs[: links.count], refs[links.count : 2 * links.count]
     qbd, fk, fv, *work = refs[2 * links.count :]
     acc = work[-1]
@@ -343,7 +346,7 @@
             else:
                 pl.when(rank[j] < CAP)(put)
         attend_list(
-            CAP, chunk, steps, (far_page, far_owner, far_limit), count,
+            CAP, ahead, chunk, steps, (far_page, far_owner, far_limit), count,
             buf, qbd, fk, fv, *work,
         )
         for j in range(links.count):
@@ -388,26 +391,27 @@
     move_cols = moves.T
     count = links.count
     chunk = 4
-    far_chunk = 5
-    fetches = math.gcd(slots, 4)
+    far_chunk = 6
+    part = math.gcd(slots, 4)
     mib = 1024 * 1024
 
-    *packed, branch = pl.pallas_call(
-        functools.partial(pack_kernel, links),
+    *packed, branch, begun = pl.pallas_call(
+        functools.partial(pack_kernel, links, part),
         out_shape=[jax.ShapeDtypeStruct((heads + fresh_rows, HD), bf16)] * count
-        + [SMEM((1,), i32)],
-        in_specs=[hbm, hbm, hbm],
-        out_specs=[vmem] * count + [smem],
+        + [SMEM((1,), i32), VMEM(kv_pool.shape, bf16)],
+        in_specs=[hbm] * 4,
+        out_specs=[vmem] * count + [smem, vmem],
         scratch_shapes=[
             SMEM((count + 1,), i32),
             SMEM(move_cols.shape, i32),
             VMEM(q.shape, bf16),
             VMEM(kv.shape, bf16),
             pltpu.SemaphoreType.DMA((3,)),
+            pltpu.SemaphoreType.DMA((1, 2)),
         ],
         compiler_params=pltpu.CompilerParams(vmem_limit_bytes=4 * mib),
         name="pack",
-    )(in_hbm(move_cols), in_hbm(q), in_hbm(kv))
+    )(*map(in_hbm, (move_cols, q, kv, kv_pool)))
 
     def rows_state(rows):
         return [
@@ -427,23 +431,23 @@
     staged = VMEM((rows_inst, heads, HD), bf16)
 
     def exchange(arrays, ways):
-        done = {j: lax.ppermute(arrays[j], "inst", ways[j]) for j in reversed(range(count))}
-        return [done[j] for j in range(count)]
-
-    def rest(which, kv_pool, page_table, lengths, q, kv, move_cols, *packed):
+        return [lax.ppermute(x, "inst", way) for x, way in zip(arrays, ways)]
+
+    def rest(which, kv_pool, page_table, lengths, q, kv, move_cols, begun, *packed):
         ways = [links.forward(which, j) for j in range(count)]
         received = exchange(packed, [links.both(way) for way in ways])
         (
             buf, qbd, fk, fv, hidden, rank, slot,
             page, owner, limit, counts, far_page, far_owner, far_limit,
         ) = pl.pallas_call(
-            functools.partial(list_kernel, links, chunk, far_chunk, fetches),
+            functools.partial(list_kernel, links, chunk, far_chunk, part),
             out_shape=[VMEM(kv_pool.shape, bf16)]
             + rows_state(rows_inst)
             + [SMEM((count + 1,), i32), SMEM((count + 1,), i32), SMEM((CAP + 1,), i32)]
             + [blocks, blocks, blocks, SMEM((2,), i32), blocks, blocks, blocks],
-            in_specs=[hbm] * 6,
+            in_specs=[hbm] * 6 + [vmem],
             out_specs=[vmem] * 4 + [smem] * 10,
+            input_output_aliases={6: 0},
             scratch_shapes=[
                 SMEM(move_cols.shape, i32),
                 SMEM(page_table.shape, i32),
@@ -451,14 +455,14 @@
                 VMEM(q.shape, bf16),
                 VMEM(kv.shape, bf16),
                 pltpu.SemaphoreType.DMA((5,)),
-                pltpu.SemaphoreType.DMA((fetches, 2)),
+                pltpu.SemaphoreType.DMA((slots // part, 2)),
             ],
             compiler_params=pltpu.CompilerParams(vmem_limit_bytes=16 * mib),
             cost_estimate=pl.CostEstimate(flops=2**27, bytes_accessed=2**23, transcendentals=2**18),
             name="list",
-        )(*map(in_hbm, (move_cols, page_table, lengths, q, kv, kv_pool)))
+        )(*map(in_hbm, (move_cols, page_table, lengths, q, kv, kv_pool)), begun)
         back = pl.pallas_call(
-            functools.partial(moved_kernel, links, far_chunk, steps),
+            functools.partial(moved_kernel, links, chunk, far_chunk, steps),
             out_shape=[jax.ShapeDtypeStruct((heads, HD), bf16)] * count,
             in_specs=[smem] * 5 + [vmem] + [vmem] * count,
             out_specs=[vmem] * count,
@@ -489,7 +493,7 @@
         out = out.reshape(rows_inst, heads_all, steps, HD).transpose(0, 2, 1, 3)
         return out.reshape(rows_inst, steps, width)
 
-    operands = (kv_pool, page_table, lengths, q, kv, move_cols, *packed)
+    operands = (kv_pool, page_table, lengths, q, kv, move_cols, begun, *packed)
     if links.split:
         return lax.switch(
             branch[0], [functools.partial(rest, k) for k in range(len(links.halves))], *operands

time: 20.2 us -> 20.6 us (1.020); the launches traced: 20.4 us -> 20.3 us
  starting transfers between devices: 8.02 us -> 7.69 us
    ppermute x4, starting transfers between devices: 8.02 us -> 7.69 us  [exchange(): return [lax.ppermute(x, 'inst', way) for x, way in zip(arrays, ways)]]
  transfers between devices with their start and end apart: 4 -> 4, of which waited for: 3 -> 3; matrix products, arithmetic and copies ran while one was open for 0% -> 0% of each run, Pallas kernels for 27% -> 24%
where the time goes in v1:
time: 20.6 us; the launch traced here: 20.3 us
  starting transfers between devices  7.69 us (37%)
  Pallas kernels  7.18 us (35%)
  waiting for transfers between devices  4.79 us (23%)
  loops' own time  0.49 us (2%)
    ppermute x4, starting transfers between devices, exchange(): return [lax.ppermute(x, 'inst', way) for x, way in zip(arrays, ways)]  7.69 us
    ppermute x4, waiting for transfers between devices, exchange(): return [lax.ppermute(x, 'inst', way) for x, way in zip(arrays, ways)]  4.79 us
    pallas_call x1, Pallas kernels, rest(): pl.pallas_call(functools.partial(list_kernel, links, chunk, far_chunk, pa...  3.02 us
    pallas_call x1, Pallas kernels, rest(): pl.pallas_call(functools.partial(stay_kernel, chunk, steps), out_shape=st...  1.88 us
    pallas_call x1, Pallas kernels, body(): pl.pallas_call(functools.partial(pack_kernel, links, part), out_shape=[ja...  1.64 us
    pallas_call x1, Pallas kernels, rest(): pl.pallas_call(functools.partial(place_kernel, links), out_shape=HBM((row...  0.64 us
    another operation x1, loops' own time, body(): lax.switch(branch[0], [functools.partial(rest, k) for k in range(len(link...  0.49 us
  transfers between devices with their start and end apart: 4, of which 3 were waited for; matrix products, arithmetic and copies ran while one was open for 0% of the time, Pallas kernels for 24%

profile of v1, /device:TPU:0, one launch (start us, length us, event | category | flops | bytes accessed | tf_op | source)
XLA Modules:
  0.0 20.3 jit_solution(8446173248938329493)
XLA Ops:
  0.0 1.6 %pack.1 = (bf16[40,128]{1,0:T(8,128)(2,1)S(1)}, bf16[40,128]{1,0:T(8,128)(2,1)S(1)}, s32[1]{0:T(128)S(4)}, bf16[16,2,512,256]{3,2,1,0:T(8,128)(2,1)S(1)}) custom-call(s32[2,4]{1,0:T(2,128)} %bitcast.62, bf16[8,32,128]{2,1,0:T(8,128)(2,1)} %bitcast.42, bf16[8,8,128]{2,1,0:T(8,128)(2,1)} %bitcast.49, bf16[16,2,512,256]{3,2,1,0:T(8,128)(2,1)} %pool.1), custom_call_target="tpu_custom_call" | custom-call | tf_op jit(solution)/shard_map/pack/pallas_call | solution.py:398
  1.7 18.5 %conditional.1 = (bf16[8,2,2048]{2,1,0:T(2,128)(2,1)}) conditional(s32[]{:T(128)} %bitcast.37, (s32[2,4]{1,0:T(2,128)}, s32[8,8]{1,0:T(8,128)}, s32[8]{0:T(128)}, bf16[8,32,128]{2,1,0:T(8,128)(2,1)}, bf16[8,8,128]{2,1,0:T(8,128)(2,1)}, /*index=5*/bf16[16,2,512,256]{3,2,1,0:T(8,128)(2,1)}, ...), branch_computations={%region_0.0_spmd, %region_1.0_spmd, %region_2.0_spmd, %region_3.0_... | conditional | flops 268435456 | bytes 16924840 | solution.py:498
  1.9 5.1 %collective-permute-start.20 = (bf16[40,128]{1,0:T(8,128)(2,1)S(1)}, bf16[40,128]{1,0:T(8,128)(2,1)S(1)}, u32[]{:S(2)}, u32[]{:S(2)}) collective-permute-start(bf16[40,128]{1,0:T(8,128)(2,1)S(1)} %get-tuple-element.266), channel_id=1, source_target_pairs={{0,12},{4,8},{8,4},{12,0},{1,13},{5,9},{9,5},{13,1},{2,14},{6,10},... | collective-permute-start | bytes 30728 | tf_op jit(solution)/shard_map/cond/branch_5_fun/ppermute | solution.py:434
  7.0 0.0 collective-permute-start.21
  7.0 3.0 %list.11 = (bf16[16,2,512,256]{3,2,1,0:T(8,128)(2,1)S(1)}, bf16[9,32,256]{2,1,0:T(8,128)(2,1)S(1)}, bf16[8,128,256]{2,1,0:T(8,128)(2,1)S(1)}, bf16[8,128,256]{2,...) custom-call(s32[2,4]{1,0:T(2,128)} %get-tuple-element.245.moves_hbm,, ...), custom_call_target="tpu_custom_call", output_to_operand_aliasing={{0}: (6, {})} | custom-call | flops 134217728 | bytes 8388608 | tf_op jit(solution)/shard_map/cond/branch_5_fun/list/pallas_call | solution.py:442
  10.0 0.0 collective-permute-done.20.refs_0_
  10.0 1.5 %collective-permute-done.21.refs_1_ = bf16[40,128]{1,0:T(8,128)(2,1)S(1)} collective-permute-done((bf16[40,128]{1,0:T(8,128)(2,1)S(1)}, bf16[40,128]{1,0:T(8,128)(2,1)S(1)}, u32[]{:S(2)}, u32[]{:S(2)}) %collective-permute-start.21) | collective-permute-done | bytes 10272 | tf_op jit(solution)/shard_map/cond/branch_5_fun/ppermute | solution.py:434
  11.6 1.3 %collective-permute-start.22 = (bf16[32,128]{1,0:T(8,128)(2,1)S(1)}, bf16[32,128]{1,0:T(8,128)(2,1)S(1)}, u32[]{:S(2)}, u32[]{:S(2)}) collective-permute-start(bf16[32,128]{1,0:T(8,128)(2,1)S(1)} %get-tuple-element.268.order), channel_id=1, source_target_pairs={{12,0},{8,4},{13,1},{9,5},{14,2},{10,6},{15,3},{11,7},{28,16},{24,... | collective-permute-start | bytes 24584 | tf_op jit(solution)/shard_map/cond/branch_5_fun/ppermute | solution.py:434
  12.9 1.3 %collective-permute-start.23 = (bf16[32,128]{1,0:T(8,128)(2,1)S(1)}, bf16[32,128]{1,0:T(8,128)(2,1)S(1)}, u32[]{:S(2)}, u32[]{:S(2)}) collective-permute-start(bf16[32,128]{1,0:T(8,128)(2,1)S(1)} %get-tuple-element.269), channel_id=1, source_target_pairs={{8,0},{12,4},{9,1},{13,5},{10,2},{14,6},{11,3},{15,7},{24,16},{28,... | collective-permute-start | bytes 24584 | tf_op jit(solution)/shard_map/cond/branch_5_fun/ppermute | solution.py:434
  14.2 1.9 %stay.11.local = bf16[8,32,128]{2,1,0:T(8,128)(2,1)S(1)} custom-call(s32[3]{0:T(128)S(4)} %get-tuple-element.253.slot, s32[23]{0:T(128)S(4)} %get-tuple-element.254.page, s32[23]{0:T(128)S(4)} %get-tuple-element.255.owner, s32[23]{0:T(128)S(4)} %get-tuple-element.256.limit, s32[2]{0:T(128)S(4)} %get-tuple-element.257.counts, ...), custom_call_target="tpu_custom_call" | custom-call | flops 134217728 | bytes 8388608 | tf_op jit(solution)/shard_map/cond/branch_5_fun/stay/pallas_call | solution.py:474
  16.0 2.9 %collective-permute-done.22.refs_0_ = bf16[32,128]{1,0:T(8,128)(2,1)S(1)} collective-permute-done((bf16[32,128]{1,0:T(8,128)(2,1)S(1)}, bf16[32,128]{1,0:T(8,128)(2,1)S(1)}, u32[]{:S(2)}, u32[]{:S(2)}) %collective-permute-start.22) | collective-permute-done | bytes 8224 | tf_op jit(solution)/shard_map/cond/branch_5_fun/ppermute | solution.py:434
  18.9 0.4 %collective-permute-done.23.refs_1_ = bf16[32,128]{1,0:T(8,128)(2,1)S(1)} collective-permute-done((bf16[32,128]{1,0:T(8,128)(2,1)S(1)}, bf16[32,128]{1,0:T(8,128)(2,1)S(1)}, u32[]{:S(2)}, u32[]{:S(2)}) %collective-permute-start.23) | collective-permute-done | bytes 8224 | tf_op jit(solution)/shard_map/cond/branch_5_fun/ppermute | solution.py:434
  19.3 0.6 %place.11 = bf16[8,32,128]{2,1,0:T(8,128)(2,1)} custom-call(s32[3]{0:T(128)S(4)} %get-tuple-element.252.hidden, bf16[8,32,128]{2,1,0:T(8,128)(2,1)S(1)} %stay.11.local, bf16[32,128]{1,0:T(8,128)(2,1)S(1)} %collective-permute-done.22.refs_0_, bf16[32,128]{1,0:T(8,128)(2,1)S(1)} %collective-permute-done.23.refs_1_), custom_call_target="tpu_custom_call" | custom-call | tf_op jit(solution)/shard_map/cond/branch_5_fun/place/pallas_call | solution.py:484
  (1 shorter events, 0.0 us)
Async XLA Ops:
  1.9 8.1 %collective-permute-start.20 = (bf16[40,128]{1,0:T(8,128)(2,1)S(1)}, bf16[40,128]{1,0:T(8,128)(2,1)S(1)}, u32[]{:S(2)}, u32[]{:S(2)}) collective-permute-start(bf16[40,128]{1,0:T(8,128)(2,1)S(1)} %get-tuple-element.266), channel_id=1, source_target_pairs={{0,12},{4,8},{8,4},{12,0},{1,13},{5,9},{9,5},{13,1},{2,14},{6,10},... | collective-permute-start | bytes 30728 | tf_op jit(solution)/shard_map/cond/branch_5_fun/ppermute | solution.py:434
  7.0 4.6 %collective-permute-start.21 = (bf16[40,128]{1,0:T(8,128)(2,1)S(1)}, bf16[40,128]{1,0:T(8,128)(2,1)S(1)}, u32[]{:S(2)}, u32[]{:S(2)}) collective-permute-start(bf16[40,128]{1,0:T(8,128)(2,1)S(1)} %get-tuple-element.267), channel_id=1, source_target_pairs={{0,8},{4,12},{8,0},{12,4},{1,9},{5,13},{9,1},{13,5},{2,10},{6,14},... | collective-permute-start | bytes 30728 | tf_op jit(solution)/shard_map/cond/branch_5_fun/ppermute | solution.py:434
  11.6 7.3 %collective-permute-start.22 = (bf16[32,128]{1,0:T(8,128)(2,1)S(1)}, bf16[32,128]{1,0:T(8,128)(2,1)S(1)}, u32[]{:S(2)}, u32[]{:S(2)}) collective-permute-start(bf16[32,128]{1,0:T(8,128)(2,1)S(1)} %get-tuple-element.268.order), channel_id=1, source_target_pairs={{12,0},{8,4},{13,1},{9,5},{14,2},{10,6},{15,3},{11,7},{28,16},{24,... | collective-permute-start | bytes 24584 | tf_op jit(solution)/shard_map/cond/branch_5_fun/ppermute | solution.py:434
  12.9 6.4 %collective-permute-start.23 = (bf16[32,128]{1,0:T(8,128)(2,1)S(1)}, bf16[32,128]{1,0:T(8,128)(2,1)S(1)}, u32[]{:S(2)}, u32[]{:S(2)}) collective-permute-start(bf16[32,128]{1,0:T(8,128)(2,1)S(1)} %get-tuple-element.269), channel_id=1, source_target_pairs={{8,0},{12,4},{9,1},{13,5},{10,2},{14,6},{11,3},{15,7},{24,16},{28,... | collective-permute-start | bytes 24584 | tf_op jit(solution)/shard_map/cond/branch_5_fun/ppermute | solution.py:434

commit v2 on v0

--- a/solution.py
+++ b/solution.py
@@ -150,7 +150,7 @@
             ref[at, 0:16, g * hd : (g + 1) * hd] = block.astype(jnp.bfloat16)
 
 
-def attend_list(rows, chunk, steps, lists, count, buf, qbd, fk, fv, scores, new, part_max, top, part_sum, acc):
+def attend_list(rows, ahead, chunk, steps, lists, count, buf, qbd, fk, fv, scores, new, part_max, top, part_sum, acc):
     page, owner, limit = lists
     _, heads, columns = qbd.shape
     hd = acc.shape[2]
@@ -158,7 +158,7 @@
     per = heads // groups
     block = buf.shape[2]
     factor = math.log2(math.e) / math.sqrt(hd)
-    loops = lax.div(count + (chunk - 1), jnp.int32(chunk))
+    loops = lax.div(count - ahead + (chunk - 1), jnp.int32(chunk))
     keys_of = (((1,), (1,)), ((), ()))
     values_of = (((1,), (0,)), ((), ()))
     lane = lax.broadcasted_iota(jnp.int32, (heads, block), 1)
@@ -198,10 +198,10 @@
     def others(do):
         def step(i, carry):
             for j in range(chunk):
-                do(i * chunk + j)
+                do(ahead + i * chunk + j)
             return carry
 
-        lax.fori_loop(1, loops, step, 0)
+        lax.fori_loop(0, loops, step, 0)
 
     for r in range(rows):
         s = lax.dot_general(qbd[r], fk[r], keys_of, preferred_element_type=jnp.float32)
@@ -209,7 +209,7 @@
         new[r] = s
         part_max[r] = s
     part_max[rows] = jnp.zeros((heads, hd), jnp.float32)
-    for j in range(chunk):
+    for j in range(ahead):
         first(j)
     others(first)
 
@@ -224,7 +224,7 @@
         acc[r] = diagonal(
             lax.dot_general(e.astype(jnp.bfloat16), fv[r], values_of, preferred_element_type=jnp.float32)
         )
-    for j in range(chunk):
+    for j in range(ahead):
         second(j)
     others(second)
     for r in range(rows):
@@ -314,14 +314,14 @@
 
 def stay_kernel(chunk, steps, slot, page, owner, limit, counts, buf, qbd, fk, fv, order, local, *work):
     rows_inst = local.shape[0]
-    attend_list(rows_inst, chunk, steps, (page, owner, limit), counts[0], buf, qbd, fk, fv, *work)
+    attend_list(rows_inst, chunk, chunk, steps, (page, owner, limit), counts[0], buf, qbd, fk, fv, *work)
     acc = work[-1]
     for r in range(rows_inst):
         vacant = functools.reduce(jnp.logical_or, [slot[c] == r for c in range(CAP)])
         local[r] = jnp.where(vacant, 0.0, acc[r]).astype(jnp.bfloat16)
 
 
-def moved_kernel(links, chunk, steps, rank, far_page, far_owner, far_limit, counts, buf, *refs):
+def moved_kernel(links, ahead, chunk, steps, rank, far_page, far_owner, far_limit, counts, buf, *refs):
     recv, back = refs[: links.count], refs[links.count : 2 * links.count]
     qbd, fk, fv, *work = refs[2 * links.count :]
     acc = work[-1]
@@ -343,11 +343,11 @@
             else:
                 pl.when(rank[j] < CAP)(put)
         attend_list(
-            CAP, chunk, steps, (far_page, far_owner, far_limit), count,
+            CAP, ahead, chunk, steps, (far_page, far_owner, far_limit), count,
             buf, qbd, fk, fv, *work,
         )
-        for j in range(links.count):
-            back[j][...] = acc[rank[j]].astype(jnp.bfloat16)
+        for out, j in zip(back, reversed(range(links.count))):
+            out[...] = acc[rank[j]].astype(jnp.bfloat16)
 
 
 def place_kernel(links, hidden, local, *refs):
@@ -388,7 +388,7 @@
     move_cols = moves.T
     count = links.count
     chunk = 4
-    far_chunk = 5
+    far_chunk = 6
     fetches = math.gcd(slots, 4)
     mib = 1024 * 1024
 
@@ -426,13 +426,9 @@
     blocks = SMEM((slots + far_chunk + 1,), i32)
     staged = VMEM((rows_inst, heads, HD), bf16)
 
-    def exchange(arrays, ways):
-        done = {j: lax.ppermute(arrays[j], "inst", ways[j]) for j in reversed(range(count))}
-        return [done[j] for j in range(count)]
-
     def rest(which, kv_pool, page_table, lengths, q, kv, move_cols, *packed):
         ways = [links.forward(which, j) for j in range(count)]
-        received = exchange(packed, [links.both(way) for way in ways])
+        received = [lax.ppermute(x, "inst", links.both(way)) for x, way in zip(packed, ways)]
         (
             buf, qbd, fk, fv, hidden, rank, slot,
             page, owner, limit, counts, far_page, far_owner, far_limit,
@@ -458,7 +454,7 @@
             name="list",
         )(*map(in_hbm, (move_cols, page_table, lengths, q, kv, kv_pool)))
         back = pl.pallas_call(
-            functools.partial(moved_kernel, links, far_chunk, steps),
+            functools.partial(moved_kernel, links, chunk, far_chunk, steps),
             out_shape=[jax.ShapeDtypeStruct((heads, HD), bf16)] * count,
             in_specs=[smem] * 5 + [vmem] + [vmem] * count,
             out_specs=[vmem] * count,
@@ -466,7 +462,10 @@
             compiler_params=pltpu.CompilerParams(vmem_limit_bytes=16 * mib),
             name="moved",
         )(rank, far_page, far_owner, far_limit, counts, buf, *received)
-        returned = exchange(back, [links.backward(which, j) for j in range(count)])
+        ways = [links.backward(which, j) for j in range(count)]
+        ways[0] = links.both(ways[0])
+        returned = [lax.ppermute(x, "inst", way) for x, way in zip(back, reversed(ways))]
+        returned.reverse()
         local = pl.pallas_call(
             functools.partial(stay_kernel, chunk, steps),
             out_shape=staged,

time: 20.2 us -> 20 us (0.990)
  waiting for transfers between devices: 4.63 us -> 0.5 us
  Pallas kernels: 7.03 us -> 9.49 us
  starting transfers between devices: 8.02 us -> 9.54 us
    ppermute x4, waiting for transfers between devices: 4.63 us -> 0.5 us  [the longest x2 0.5 us: rest(): lax.ppermute(x, 'inst', links.both(way))]
    ppermute x4, starting transfers between devices: 8.02 us -> 9.54 us  [the longest x2 5.45 us: rest(): lax.ppermute(x, 'inst', links.both(way))]
    pallas_call x1, Pallas kernels: 1.91 us -> 3.36 us  [rest(): pl.pallas_call(functools.partial(stay_kernel, chunk, steps), out_shape=st...]
    pallas_call x1, Pallas kernels: 0.01 us -> 0.99 us  [rest(): pl.pallas_call(functools.partial(moved_kernel, links, chunk, far_chunk, s...]
  transfers between devices with their start and end apart: 4 -> 4, of which waited for: 3 -> 1; matrix products, arithmetic and copies ran while one was open for 0% -> 0% of each run, Pallas kernels for 27% -> 35%
where the time goes in v2:
time: 20 us
  starting transfers between devices  9.54 us (48%)
  Pallas kernels  9.49 us (47%)
  waiting for transfers between devices  0.5 us (2%)
  loops' own time  0.31 us (2%)
    ppermute x2, starting transfers between devices, rest(): lax.ppermute(x, 'inst', links.both(way))  5.45 us
    ppermute x2, starting transfers between devices, rest(): lax.ppermute(x, 'inst', way)  4.09 us
    pallas_call x1, Pallas kernels, rest(): pl.pallas_call(functools.partial(list_kernel, links, chunk, far_chunk, fe...  3.61 us
    pallas_call x1, Pallas kernels, rest(): pl.pallas_call(functools.partial(stay_kernel, chunk, steps), out_shape=st...  3.36 us
    pallas_call x1, Pallas kernels, rest(): pl.pallas_call(functools.partial(moved_kernel, links, chunk, far_chunk, s...  0.99 us
    pallas_call x1, Pallas kernels, body(): pl.pallas_call(functools.partial(pack_kernel, links), out_shape=[jax.Shap...  0.87 us
    pallas_call x1, Pallas kernels, rest(): pl.pallas_call(functools.partial(place_kernel, links), out_shape=HBM((row...  0.66 us
    ppermute x2, waiting for transfers between devices, rest(): lax.ppermute(x, 'inst', links.both(way))  0.5 us
  transfers between devices with their start and end apart: 4, of which 1 were waited for; matrix products, arithmetic and copies ran while one was open for 0% of the time, Pallas kernels for 35%

profile of v2, /device:TPU:0, one launch (start us, length us, event | category | flops | bytes accessed | tf_op | source)
XLA Modules:
  0.0 20.0 jit_solution(13113403727231231956)
XLA Ops:
  0.0 0.9 %pack.1 = (bf16[40,128]{1,0:T(8,128)(2,1)S(1)}, bf16[40,128]{1,0:T(8,128)(2,1)S(1)}, s32[1]{0:T(128)S(4)}) custom-call(s32[2,4]{1,0:T(2,128)} %bitcast.62, bf16[8,32,128]{2,1,0:T(8,128)(2,1)} %bitcast.42, bf16[8,8,128]{2,1,0:T(8,128)(2,1)} %bitcast.49), custom_call_target="tpu_custom_call" | custom-call | tf_op jit(solution)/shard_map/pack/pallas_call | solution.py:395
  0.9 19.0 %conditional.1 = (bf16[8,2,2048]{2,1,0:T(2,128)(2,1)}) conditional(s32[]{:T(128)} %bitcast.37, (s32[2,4]{1,0:T(2,128)}, s32[8,8]{1,0:T(8,128)}, s32[8]{0:T(128)}, bf16[8,32,128]{2,1,0:T(8,128)(2,1)}, bf16[8,8,128]{2,1,0:T(8,128)(2,1)}, /*index=5*/bf16[16,2,512,256]{3,2,1,0:T(8,128)(2,1)}, ...), branch_computations={%region_0.0_spmd, %region_1.0_spmd, %region_2.0_spmd, %region_3.0_... | conditional | flops 268435456 | bytes 16924840 | solution.py:493
  0.9 4.1 %collective-permute-start = (bf16[40,128]{1,0:T(8,128)(2,1)S(1)}, bf16[40,128]{1,0:T(8,128)(2,1)S(1)}, u32[]{:S(2)}, u32[]{:S(2)}) collective-permute-start(bf16[40,128]{1,0:T(8,128)(2,1)S(1)} %get-tuple-element.128), channel_id=1, source_target_pairs={{0,8},{4,12},{8,0},{12,4},{1,9},{5,13},{9,1},{13,5},{2,10},{6,14},... | collective-permute-start | bytes 30728 | tf_op jit(solution)/shard_map/cond/branch_0_fun/ppermute | solution.py:431
  5.0 1.3 %collective-permute-start.1 = (bf16[40,128]{1,0:T(8,128)(2,1)S(1)}, bf16[40,128]{1,0:T(8,128)(2,1)S(1)}, u32[]{:S(2)}, u32[]{:S(2)}) collective-permute-start(bf16[40,128]{1,0:T(8,128)(2,1)S(1)} %get-tuple-element.129), channel_id=1, source_target_pairs={{0,12},{4,8},{8,4},{12,0},{1,13},{5,9},{9,5},{13,1},{2,14},{6,10},... | collective-permute-start | bytes 30728 | tf_op jit(solution)/shard_map/cond/branch_0_fun/ppermute | solution.py:431
  6.4 3.6 %list.6 = (bf16[16,2,512,256]{3,2,1,0:T(8,128)(2,1)S(1)}, bf16[9,32,256]{2,1,0:T(8,128)(2,1)S(1)}, bf16[8,128,256]{2,1,0:T(8,128)(2,1)S(1)}, bf16[8,128,256]{2,1...) custom-call(s32[2,4]{1,0:T(2,128)} %get-tuple-element.96.moves_hbm, ...), custom_call_target="tpu_custom_call" | custom-call | flops 134217728 | bytes 8388608 | tf_op jit(solution)/shard_map/cond/branch_0_fun/list/pallas_call | solution.py:435
  10.0 0.0 collective-permute-done.refs_0_
  10.0 0.5 %collective-permute-done.1.refs_1_ = bf16[40,128]{1,0:T(8,128)(2,1)S(1)} collective-permute-done((bf16[40,128]{1,0:T(8,128)(2,1)S(1)}, bf16[40,128]{1,0:T(8,128)(2,1)S(1)}, u32[]{:S(2)}, u32[]{:S(2)}) %collective-permute-start.1) | collective-permute-done | bytes 10272 | tf_op jit(solution)/shard_map/cond/branch_0_fun/ppermute | solution.py:431
  10.5 1.0 %moved.6 = (bf16[32,128]{1,0:T(8,128)(2,1)S(1)}, bf16[32,128]{1,0:T(8,128)(2,1)S(1)}) custom-call(s32[3]{0:T(128)S(4)} %get-tuple-element.124.rank, s32[23]{0:T(128)S(4)} %get-tuple-element.125.far_page, s32[23]{0:T(128)S(4)} %get-tuple-element.126.far_owner, s32[23]{0:T(128)S(4)} %get-tuple-element.127.far_limit, s32[2]{0:T(128)S(4)} %get-tuple-element.119.counts, ...), custom_call_target="tpu_custom_call" | custom-call | tf_op jit(solution)/shard_map/cond/branch_0_fun/moved/pallas_call | solution.py:456
  11.5 0.3 %collective-permute-start.2 = (bf16[32,128]{1,0:T(8,128)(2,1)S(1)}, bf16[32,128]{1,0:T(8,128)(2,1)S(1)}, u32[]{:S(2)}, u32[]{:S(2)}) collective-permute-start(bf16[32,128]{1,0:T(8,128)(2,1)S(1)} %get-tuple-element.131), channel_id=1, source_target_pairs={{0,8},{4,12},{8,0},{12,4},{1,9},{5,13},{9,1},{13,5},{2,10},{6,14},... | collective-permute-start | bytes 24584 | tf_op jit(solution)/shard_map/cond/branch_0_fun/ppermute | solution.py:467
  11.8 3.8 %collective-permute-start.3 = (bf16[32,128]{1,0:T(8,128)(2,1)S(1)}, bf16[32,128]{1,0:T(8,128)(2,1)S(1)}, u32[]{:S(2)}, u32[]{:S(2)}) collective-permute-start(bf16[32,128]{1,0:T(8,128)(2,1)S(1)} %get-tuple-element.130.order), channel_id=1, source_target_pairs={{4,8},{0,12},{5,9},{1,13},{6,10},{2,14},{7,11},{3,15},{20,24},{16,... | collective-permute-start | bytes 24584 | tf_op jit(solution)/shard_map/cond/branch_0_fun/ppermute | solution.py:467
  15.6 3.4 %stay.6.local = bf16[8,32,128]{2,1,0:T(8,128)(2,1)S(1)} custom-call(s32[3]{0:T(128)S(4)} %get-tuple-element.115.slot, s32[23]{0:T(128)S(4)} %get-tuple-element.116.page, s32[23]{0:T(128)S(4)} %get-tuple-element.117.owner, s32[23]{0:T(128)S(4)} %get-tuple-element.118.limit, s32[2]{0:T(128)S(4)} %get-tuple-element.119.counts, ...), custom_call_target="tpu_custom_call" | custom-call | flops 134217728 | bytes 8388608 | tf_op jit(solution)/shard_map/cond/branch_0_fun/stay/pallas_call | solution.py:469
  18.9 0.0 collective-permute-done.2.refs_0_
  19.0 0.0 collective-permute-done.3.refs_1_
  19.0 0.7 %place.6 = bf16[8,32,128]{2,1,0:T(8,128)(2,1)} custom-call(s32[3]{0:T(128)S(4)} %get-tuple-element.114.hidden, bf16[8,32,128]{2,1,0:T(8,128)(2,1)S(1)} %stay.6.local, bf16[32,128]{1,0:T(8,128)(2,1)S(1)} %collective-permute-done.2.refs_0_, bf16[32,128]{1,0:T(8,128)(2,1)S(1)} %collective-permute-done.3.refs_1_), custom_call_target="tpu_custom_call" | custom-call | tf_op jit(solution)/shard_map/cond/branch_0_fun/place/pallas_call | solution.py:479
Async XLA Ops:
  0.9 9.1 %collective-permute-start = (bf16[40,128]{1,0:T(8,128)(2,1)S(1)}, bf16[40,128]{1,0:T(8,128)(2,1)S(1)}, u32[]{:S(2)}, u32[]{:S(2)}) collective-permute-start(bf16[40,128]{1,0:T(8,128)(2,1)S(1)} %get-tuple-element.128), channel_id=1, source_target_pairs={{0,8},{4,12},{8,0},{12,4},{1,9},{5,13},{9,1},{13,5},{2,10},{6,14},... | collective-permute-start | bytes 30728 | tf_op jit(solution)/shard_map/cond/branch_0_fun/ppermute | solution.py:431
  5.0 5.5 %collective-permute-start.1 = (bf16[40,128]{1,0:T(8,128)(2,1)S(1)}, bf16[40,128]{1,0:T(8,128)(2,1)S(1)}, u32[]{:S(2)}, u32[]{:S(2)}) collective-permute-start(bf16[40,128]{1,0:T(8,128)(2,1)S(1)} %get-tuple-element.129), channel_id=1, source_target_pairs={{0,12},{4,8},{8,4},{12,0},{1,13},{5,9},{9,5},{13,1},{2,14},{6,10},... | collective-permute-start | bytes 30728 | tf_op jit(solution)/shard_map/cond/branch_0_fun/ppermute | solution.py:431
  11.5 7.5 %collective-permute-start.2 = (bf16[32,128]{1,0:T(8,128)(2,1)S(1)}, bf16[32,128]{1,0:T(8,128)(2,1)S(1)}, u32[]{:S(2)}, u32[]{:S(2)}) collective-permute-start(bf16[32,128]{1,0:T(8,128)(2,1)S(1)} %get-tuple-element.131), channel_id=1, source_target_pairs={{0,8},{4,12},{8,0},{12,4},{1,9},{5,13},{9,1},{13,5},{2,10},{6,14},... | collective-permute-start | bytes 24584 | tf_op jit(solution)/shard_map/cond/branch_0_fun/ppermute | solution.py:467
  11.8 7.2 %collective-permute-start.3 = (bf16[32,128]{1,0:T(8,128)(2,1)S(1)}, bf16[32,128]{1,0:T(8,128)(2,1)S(1)}, u32[]{:S(2)}, u32[]{:S(2)}) collective-permute-start(bf16[32,128]{1,0:T(8,128)(2,1)S(1)} %get-tuple-element.130.order), channel_id=1, source_target_pairs={{4,8},{0,12},{5,9},{1,13},{6,10},{2,14},{7,11},{3,15},{20,24},{16,... | collective-permute-start | bytes 24584 | tf_op jit(solution)/shard_map/cond/branch_0_fun/ppermute | solution.py:467
